TPU v7x, 32 devices: a whole 2x2x4 slice. The times are simulated.
32 devices in a mesh: ctx: 8 (over z, x), tp: 4 (over y, core).
Axes of the slice: x: 2, y: 2, z: 4, core: 2. Of those that a mesh axis runs over, the one named last changes fastest.
Arguments:
- queries: bfloat16 [4096, 8192], P('ctx', 'tp'), may hold values from -23 to 23
- keys: bfloat16 [4096, 1024], P('ctx', 'tp'), may hold values from -23 to 23
- values: bfloat16 [4096, 1024], P('ctx', 'tp'), may hold values from -6 to 6
- grad_out: bfloat16 [4096, 8192], P('ctx', 'tp'), may hold values from -6 to 6
- doc_ids: int32 [4096], P(('ctx', 'tp')), may hold values from 0 to 7, never falling along the last dimension, each value on 1 to 2048 neighbouring positions
Outputs:
- attended: bfloat16 [4096, 8192], P('ctx', 'tp')
- grad_queries: bfloat16 [4096, 8192], P('ctx', 'tp')
- grad_keys: bfloat16 [4096, 1024], P('ctx', 'tp')
- grad_values: bfloat16 [4096, 1024], P('ctx', 'tp')
Inputs may be any that keep to these rules, and one draw needn't show every extreme that they name: `doc_ids`: ids never fall along the pack; each document holds 1 to 2048 tokens, one exactly 2048.
All inputs are finite; a program needn't handle non-finite values.
Results may differ from a plain program's by a relative error of at most 0.035.
Values may be sent and summed in bfloat16 or wider, within the bound.
No kernel may reach another device: no remote copies, remote signals or barrier semaphores. Data moves between devices by JAX's collectives and lax.ppermute only.
A program may use at most 128 MiB of HBM per device.

v0:
```python
import functools, math
import jax, jax.numpy as jnp
from jax import lax
from jax.sharding import PartitionSpec as P
from jax.experimental import pallas as pl
from jax.experimental.pallas import tpu as pltpu

HD = 128
KB = 256
NEG = -1e30
BIG = 1e30
F32, BF16 = jnp.float32, jnp.bfloat16


def dot(a, b):
    return lax.dot_general(a, b, (((1,), (0,)), ((), ())), preferred_element_type=F32)


def body(group, nkeys, first, lo_ref, q_ref, g_ref, kv_refs, start_ref, o_ref, dq_ref, dkv_ref,
         k_s, v_s, kt_s, vt_s, qt_s, gt_s, qs_s, gs_s, s_s, u_s, bias_s, db_s, ot_s, dqt_s, m_s, dk_s, dv_s):
    r = pl.program_id(0)
    rb = q_ref.shape[0]
    nb = nkeys // KB
    slab = kv_refs[0].shape[0]
    per = slab // KB
    c2 = math.log2(math.e) / math.sqrt(HD)

    @pl.when(r == 0)
    def _():
        for n, ref in enumerate(kv_refs):
            for t in range(per):
                j = n * per + t

                @pl.when(j >= lo_ref[0])
                def _():
                    k = ref[t * KB:(t + 1) * KB, :HD]
                    v = ref[t * KB:(t + 1) * KB, HD:]
                    k_s[j] = k
                    v_s[j] = v
                    kt_s[j] = k.T
                    vt_s[j, :HD] = v.T
                    vt_s[j, HD:] = jnp.ones((16, KB), BF16)
        dk_s[...] = jnp.zeros_like(dk_s)
        dv_s[...] = jnp.zeros_like(dv_s)

    for h in range(group):
        q = q_ref[:, h * HD:(h + 1) * HD]
        g = g_ref[:, h * HD:(h + 1) * HD]
        qs_s[h * rb:(h + 1) * rb, :] = q
        qt_s[:, h * rb:(h + 1) * rb] = q.T
        gt_s[:, h * rb:(h + 1) * rb] = g.T

    lo = lo_ref[r]
    hi = nb - pl.num_programs(0) * rb // KB + (r + 1) * rb // KB
    start = start_ref[0:1, :]
    qpos = (nkeys - pl.num_programs(0) * rb) + r * rb + lax.broadcasted_iota(jnp.int32, (1, rb), 1)
    dqt_s[...] = jnp.zeros_like(dqt_s)

    def set_bias(j):
        kpos = j * KB + lax.broadcasted_iota(jnp.int32, (KB, rb), 0)
        bias_s[...] = jnp.where((kpos >= start) & (kpos <= qpos), BIG, NEG)

    def scores(j, cols):
        return jnp.minimum(dot(k_s[j], qt_s[:, cols]), bias_s[...])

    def fold_max(s):
        return jnp.max(s.reshape(KB // 8, 8, rb), axis=0)

    def weigh(j, s, cols):
        u_s[j, :, cols] = jnp.exp2(s * c2 - m_s[0:1, cols]).astype(BF16)

    heads = [slice(h * rb, (h + 1) * rb) for h in range(group)]

    last = hi - 1
    set_bias(last)
    for cols in heads:
        s = scores(last, cols)
        s_s[:, cols] = s
        m_s[0:1, cols] = jnp.max(fold_max(s), axis=0, keepdims=True) * c2
    for cols in heads:
        weigh(last, s_s[:, cols], cols)
    ot_s[...] = dot(vt_s[last], u_s[last])

    @pl.loop(lo, last)
    def _(j):
        set_bias(j)
        for cols in heads:
            weigh(j, scores(j, cols), cols)
        ot_s[...] += dot(vt_s[j], u_s[j])

    @pl.when(jnp.logical_not(jnp.max(ot_s[HD:HD + 1, :]) < 2.0 ** 60))
    def _():
        m_s[...] = jnp.full_like(m_s, NEG)

        @pl.loop(lo, hi)
        def _(j):
            set_bias(j)
            for cols in heads:
                m_s[:, cols] = jnp.maximum(m_s[:, cols], fold_max(scores(j, cols)))

        m_s[0:1, :] = jnp.max(m_s[...], axis=0, keepdims=True) * c2
        ot_s[...] = jnp.zeros_like(ot_s)

        @pl.loop(lo, hi)
        def _(j):
            set_bias(j)
            for cols in heads:
                weigh(j, scores(j, cols), cols)
            ot_s[...] += dot(vt_s[j], u_s[j])

    rl = 1.0 / ot_s[HD:HD + 1, :]
    deltas = []
    for h in range(group):
        cols = slice(h * rb, (h + 1) * rb)
        ob = (ot_s[:HD, cols] * rl[:, cols]).astype(BF16)
        o_ref[:, h * HD:(h + 1) * HD] = ob.T
        gt = gt_s[:, cols].astype(F32) * rl[:, cols]
        deltas.append(jnp.sum(ob.astype(F32) * gt, axis=0, keepdims=True))
        gt = gt.astype(BF16)
        gt_s[:, cols] = gt
        gs_s[h * rb:(h + 1) * rb, :] = gt.T

    @pl.loop(lo, hi)
    def _(j):
        vj = v_s[j]
        for h in range(group):
            cols = slice(h * rb, (h + 1) * rb)
            dp = dot(vj, gt_s[:, cols])
            db_s[:, cols] = (u_s[j, :, cols].astype(F32) * (dp - deltas[h])).astype(BF16)
        dqt_s[...] += dot(kt_s[j], db_s[...])
        dk_s[j] += dot(db_s[...], qs_s[...])
        dv_s[j] += dot(u_s[j], gs_s[...])

    scale = 1.0 / math.sqrt(HD)
    for h in range(group):
        cols = slice(h * rb, (h + 1) * rb)
        dq_ref[:, h * HD:(h + 1) * HD] = (dqt_s[:, cols] * scale).astype(BF16).T

    @pl.when(r == pl.num_programs(0) - 1)
    def _():
        for j in range(nb):
            dkv_ref[j * KB:(j + 1) * KB, :HD] = (dk_s[j] * scale).astype(BF16)
            dkv_ref[j * KB:(j + 1) * KB, HD:] = dv_s[j].astype(BF16)


def attend(q, g, kvs, start, lo, chunk, group, prev=None, rb=256):
    rows, width = q.shape
    gw = group * HD
    slab = kvs[0].shape[0]
    nkeys = slab * len(kvs)
    nb = nkeys // KB
    R = group * rb
    n = len(kvs)

    def kernel(*refs):
        if prev is None:
            lo_ref, q_ref, g_ref, *rest = refs
        else:
            lo_ref, q_ref, g_ref, _, _, *rest = refs
        kv_refs, rest = rest[:n], rest[n:]
        body(group, nkeys, 0, lo_ref, q_ref, g_ref, kv_refs, *rest)

    blk = pl.BlockSpec((rb, gw), lambda r, lo: (r, chunk))
    extra = [] if prev is None else list(prev)
    return pl.pallas_call(
        kernel,
        grid_spec=pltpu.PrefetchScalarGridSpec(
            num_scalar_prefetch=1,
            grid=(rows // rb,),
            in_specs=[blk, blk] + [pl.BlockSpec(memory_space=pl.ANY)] * len(extra)
            + [pl.BlockSpec((slab, 2 * HD), lambda r, lo: (0, 0))] * n
            + [pl.BlockSpec((1, rb), lambda r, lo: (0, r))],
            out_specs=[blk, blk, pl.BlockSpec((nkeys, 2 * HD), lambda r, lo: (0, 0))],
            scratch_shapes=[
                pltpu.VMEM((nb, KB, HD), BF16), pltpu.VMEM((nb, KB, HD), BF16),
                pltpu.VMEM((nb, HD, KB), BF16), pltpu.VMEM((nb, HD + 16, KB), BF16),
                pltpu.VMEM((HD, R), BF16), pltpu.VMEM((HD, R), BF16),
                pltpu.VMEM((R, HD), BF16), pltpu.VMEM((R, HD), BF16),
                pltpu.VMEM((KB, R), F32), pltpu.VMEM((nb, KB, R), BF16),
                pltpu.VMEM((KB, rb), F32), pltpu.VMEM((KB, R), BF16),
                pltpu.VMEM((HD + 16, R), F32), pltpu.VMEM((HD, R), F32),
                pltpu.VMEM((8, R), F32),
                pltpu.VMEM((nb, KB, HD), F32), pltpu.VMEM((nb, KB, HD), F32),
            ],
        ),
        out_shape=[jax.ShapeDtypeStruct((rows, width), BF16), jax.ShapeDtypeStruct((rows, width), BF16),
                   jax.ShapeDtypeStruct((nkeys, 2 * HD), BF16)],
        input_output_aliases={} if prev is None else {3: 0, 4: 1},
        compiler_params=pltpu.CompilerParams(vmem_limit_bytes=56 * 1024 * 1024),
        name=f"attend{chunk}",
        cost_estimate=pl.CostEstimate(flops=40_000_000_000, bytes_accessed=10_000_000, transcendentals=0),
    )(lo, q, g, *extra, *kvs, start)
def hop(x, shift):
    count = lax.axis_size("ctx")
    return lax.ppermute(x, "ctx", [(s, s + shift) for s in range(count) if 0 <= s + shift < count])


def swap(x):
    return lax.ppermute(x, "ctx", [(s, s ^ 1) for s in range(lax.axis_size("ctx"))])


def after(x, *others):
    return lax.optimization_barrier((x,) + others)[0]


def gather_ids(doc_ids):
    tps = lax.axis_size("tp")
    ids = doc_ids[None]
    step = 1
    while step < tps:
        other = lax.ppermute(ids, "tp", [(t, t ^ step) for t in range(tps)])
        low = (lax.axis_index("tp") // step) % 2 == 0
        ids = jnp.where(low, jnp.concatenate([ids, other]), jnp.concatenate([other, ids]))
        step *= 2
    return ids.reshape(-1)


def on_device(queries, keys, values, grad_out, doc_ids):
    slab, width = keys.shape
    chunks = width // HD
    group = queries.shape[1] // width
    me = lax.axis_index("ctx")
    odd = lax.rem(me, 2) == 1
    rb = 256

    def own_part(c):
        return jnp.concatenate([keys[:, c * HD:(c + 1) * HD], values[:, c * HD:(c + 1) * HD]], axis=1)

    own = own_part(0)
    two = hop(own, 2)
    ids = gather_ids(doc_ids)
    two, ids_late = lax.optimization_barrier((two, ids))
    four = hop(two, 2)
    one = swap(jnp.where(odd, two, own))
    earlier = [jnp.where(me >= back, hop(ids, back), -1) for back in (4, 3, 2, 1)]
    four, earlier = lax.optimization_barrier((four, earlier))
    three = swap(jnp.where(odd, four, two))
    ready = (four, three)
    context = jnp.concatenate(earlier + [ids])
    start = jnp.sum((context[:, None] < ids[None, :]).astype(jnp.int32), axis=0)
    lo = start.reshape(slab // rb, rb)[:, 0] // KB
    start = start[None]
    blocks = [four, three, two, one, own]

    outs = None
    grads = []
    for c in range(chunks):
        following = None
        if c + 1 < chunks:
            own = after(own_part(c + 1), ready[0])
            two, own, _ = lax.optimization_barrier((hop(own, 2), own, ready[1]))
            following = [hop(two, 2), hop(two, 1), two, hop(own, 1), own]
        att, gq, parts = attend(queries, grad_out, blocks, start, lo, c, group, outs, rb)
        outs = (att, gq)
        four, three, two, one, own_grad = parts.reshape(5, slab, 2 * HD)
        if following is not None:
            back = [hop(four, -4), hop(three, -3), hop(two, -2), hop(one, -1)]
            grads.append([own_grad] + back)
        else:
            f32 = lambda x: x.astype(F32)
            three = after(three, *(x for part in grads for x in part))
            swap3 = f32(swap(three))
            swap1 = f32(swap(one))
            zero = jnp.zeros_like(swap3)
            four = (f32(four) + jnp.where(odd, swap3, zero)).astype(BF16)
            two = f32(two) + jnp.where(odd, swap1, swap3)
            two = (two + f32(hop(four, -2))).astype(BF16)
            grads.append([f32(own_grad) + jnp.where(odd, zero, swap1), hop(two, -2)])
        blocks = following
    sums = [sum(x.astype(F32) for x in parts) for parts in grads]
    grad_k = jnp.concatenate([x[:, :HD] for x in sums], axis=1).astype(BF16)
    grad_v = jnp.concatenate([x[:, HD:] for x in sums], axis=1).astype(BF16)
    return outs[0], outs[1], grad_k, grad_v


def solution(mesh):
    return jax.shard_map(
        on_device,
        mesh=mesh,
        in_specs=(P("ctx", "tp"), P("ctx", "tp"), P("ctx", "tp"), P("ctx", "tp"), P(("ctx", "tp"))),
        out_specs=(P("ctx", "tp"), P("ctx", "tp"), P("ctx", "tp"), P("ctx", "tp")),
        check_vma=False,
    )
```

profile of v0, /device:TPU:16, one launch (start us, length us, event | category | flops | bytes accessed | tf_op | source)
XLA Modules:
  0.0 167.2 jit_solution(6944806701472059553)
XLA Ops:
  1.9 3.5 %collective-permute-start = (bf16[512,256]{1,0:T(8,128)(2,1)S(1)}, bf16[512,256]{1,0:T(8,128)(2,1)S(1)}, u32[]{:S(2)}, u32[]{:S(2)}) collective-permute-start(bf16[512,256]{1,0:T(8,128)(2,1)S(1)} %pad_maximum_fusion.refs_7_), channel_id=1, source_target_pairs={{0,8},{4,12},{8,16},{12,20},{16,24},{20,28},{1,9},{5,13},{9,17},{1... | collective-permute-start | bytes 786440 | tf_op jit(solution)/shard_map/ppermute | solution.py:195
  7.7 2.0 %collective-permute-done.2 = s32[2,128]{1,0:T(2,128)S(1)} collective-permute-done((s32[2,128]{1,0:T(2,128)S(1)}, s32[2,128]{1,0:T(2,128)S(1)}, u32[]{:S(2)}, u32[]{:S(2)}) %collective-permute-start.2) | collective-permute-done | bytes 1056 | tf_op jit(solution)/shard_map/ppermute | solution.py:211
  9.7 3.4 %collective-permute-start.7 = (s32[512]{0:T(512)S(1)}, s32[512]{0:T(512)S(1)}, u32[]{:S(2)}, u32[]{:S(2)}) collective-permute-start(s32[512]{0:T(512)S(1)} %fusion.8), channel_id=1, source_target_pairs={{0,4},{4,8},{8,12},{12,16},{16,20},{20,24},{24,28},{1,5},{5,9},{9,... | collective-permute-start | bytes 6152 | tf_op jit(solution)/shard_map/ppermute | solution.py:195
  13.2 1.9 %collective-permute-start.6 = (s32[512]{0:T(512)S(1)}, s32[512]{0:T(512)S(1)}, u32[]{:S(2)}, u32[]{:S(2)}) collective-permute-start(s32[512]{0:T(512)S(1)} %fusion.8), channel_id=1, source_target_pairs={{0,8},{4,12},{8,16},{12,20},{16,24},{20,28},{1,9},{5,13},{9,17},{1... | collective-permute-start | bytes 6152 | tf_op jit(solution)/shard_map/ppermute | solution.py:195
  15.1 1.9 %collective-permute-start.5 = (s32[512]{0:T(512)S(1)}, s32[512]{0:T(512)S(1)}, u32[]{:S(2)}, u32[]{:S(2)}) collective-permute-start(s32[512]{0:T(512)S(1)} %fusion.8), channel_id=1, source_target_pairs={{0,12},{4,16},{8,20},{12,24},{16,28},{1,13},{5,17},{9,21},{13,25},... | collective-permute-start | bytes 6152 | tf_op jit(solution)/shard_map/ppermute | solution.py:195
  18.7 1.9 %collective-permute-start.3 = (bf16[512,256]{1,0:T(8,128)(2,1)S(1)}, bf16[512,256]{1,0:T(8,128)(2,1)S(1)}, u32[]{:S(2)}, u32[]{:S(2)}) collective-permute-start(bf16[512,256]{1,0:T(8,128)(2,1)S(1)} %collective-permute-done.refs_5_), channel_id=1, source_target_pairs={{0,8},{4,12},{8,16},{12,20},{16,24},{20,28},{1,9},{5,13},{9,17},{1... | collective-permute-start | bytes 786440 | tf_op jit(solution)/shard_map/ppermute | solution.py:195
  20.6 1.9 %collective-permute-done.5 = s32[512]{0:T(512)S(1)} collective-permute-done((s32[512]{0:T(512)S(1)}, s32[512]{0:T(512)S(1)}, u32[]{:S(2)}, u32[]{:S(2)}) %collective-permute-start.5) | collective-permute-done | bytes 2080 | tf_op jit(solution)/shard_map/ppermute | solution.py:195
  23.6 4.1 %collective-permute-done.3.refs_3_ = bf16[512,256]{1,0:T(8,128)(2,1)S(1)} collective-permute-done((bf16[512,256]{1,0:T(8,128)(2,1)S(1)}, bf16[512,256]{1,0:T(8,128)(2,1)S(1)}, u32[]{:S(2)}, u32[]{:S(2)}) %collective-permute-start.3) | collective-permute-done | bytes 262176 | tf_op jit(solution)/shard_map/ppermute | solution.py:195
  31.1 2.2 %collective-permute-start.10 = (bf16[512,256]{1,0:T(8,128)(2,1)S(1)}, bf16[512,256]{1,0:T(8,128)(2,1)S(1)}, u32[]{:S(2)}, u32[]{:S(2)}) collective-permute-start(bf16[512,256]{1,0:T(8,128)(2,1)S(1)} %pad_maximum_fusion.1.refs_9_), channel_id=1, source_target_pairs={{0,8},{4,12},{8,16},{12,20},{16,24},{20,28},{1,9},{5,13},{9,17},{1... | collective-permute-start | bytes 786440 | tf_op jit(solution)/shard_map/ppermute | solution.py:195
  34.0 6.8 %collective-permute-done.8.refs_4_ = bf16[512,256]{1,0:T(8,128)(2,1)S(1)} collective-permute-done((bf16[512,256]{1,0:T(8,128)(2,1)S(1)}, bf16[512,256]{1,0:T(8,128)(2,1)S(1)}, u32[]{:S(2)}, u32[]{:S(2)}) %collective-permute-start.8) | collective-permute-done | bytes 262176 | tf_op jit(solution)/shard_map/ppermute | solution.py:199
  40.8 2.5 %collective-permute-start.12 = (bf16[512,256]{1,0:T(8,128)(2,1)S(1)}, bf16[512,256]{1,0:T(8,128)(2,1)S(1)}, u32[]{:S(2)}, u32[]{:S(2)}) collective-permute-start(bf16[512,256]{1,0:T(8,128)(2,1)S(1)} %collective-permute-done.10.refs_7_), channel_id=1, source_target_pairs={{0,4},{4,8},{8,12},{12,16},{16,20},{20,24},{24,28},{1,5},{5,9},{9,... | collective-permute-start | bytes 786440 | tf_op jit(solution)/shard_map/ppermute | solution.py:195
  43.4 2.1 %collective-permute-start.11 = (bf16[512,256]{1,0:T(8,128)(2,1)S(1)}, bf16[512,256]{1,0:T(8,128)(2,1)S(1)}, u32[]{:S(2)}, u32[]{:S(2)}) collective-permute-start(bf16[512,256]{1,0:T(8,128)(2,1)S(1)} %collective-permute-done.10.refs_7_), channel_id=1, source_target_pairs={{0,8},{4,12},{8,16},{12,20},{16,24},{20,28},{1,9},{5,13},{9,17},{1... | collective-permute-start | bytes 786440 | tf_op jit(solution)/shard_map/ppermute | solution.py:195
  45.5 3.1 %collective-permute-start.13 = (bf16[512,256]{1,0:T(8,128)(2,1)S(1)}, bf16[512,256]{1,0:T(8,128)(2,1)S(1)}, u32[]{:S(2)}, u32[]{:S(2)}) collective-permute-start(bf16[512,256]{1,0:T(8,128)(2,1)S(1)} %pad_maximum_fusion.1.refs_9_), channel_id=1, source_target_pairs={{0,4},{4,8},{8,12},{12,16},{16,20},{20,24},{24,28},{1,5},{5,9},{9,... | collective-permute-start | bytes 786440 | tf_op jit(solution)/shard_map/ppermute | solution.py:195
  49.3 32.0 %attend0.1 = (bf16[512,2048]{1,0:T(8,128)(2,1)}, bf16[512,2048]{1,0:T(8,128)(2,1)}, bf16[2560,256]{1,0:T(8,128)(2,1)}) custom-call(s32[2]{0:T(128)} %and_select_fusion.refs_0_, bf16[512,2048]{1,0:T(8,128)(2,1)} %refs_1_.3, bf16[512,2048]{1,0:T(8,128)(2,1)} %refs_2_.3, bf16[512,256]{1,0:T(8,128)(2,1)} %copy-done.1, bf16[512,256]{1,0:T(8,128)(2,1)} %copy-done.10, ...), custom_call_target="tpu_custom_call" | custom-call | flops 40000000000 | bytes 10000000 | tf_op jit(solution)/shard_map/attend0/pallas_call | solution.py:165
  82.6 1.9 %collective-permute-start.17 = (bf16[512,256]{1,0:T(8,128)(2,1)S(1)}, bf16[512,256]{1,0:T(8,128)(2,1)S(1)}, u32[]{:S(2)}, u32[]{:S(2)}) collective-permute-start(bf16[512,256]{1,0:T(8,128)(2,1)S(1)} %get-tuple-element.36), channel_id=1, source_target_pairs={{4,0},{8,4},{12,8},{16,12},{20,16},{24,20},{28,24},{5,1},{9,5},{13... | collective-permute-start | bytes 786440 | tf_op jit(solution)/shard_map/ppermute | solution.py:195
  84.6 1.9 %collective-permute-start.16 = (bf16[512,256]{1,0:T(8,128)(2,1)S(1)}, bf16[512,256]{1,0:T(8,128)(2,1)S(1)}, u32[]{:S(2)}, u32[]{:S(2)}) collective-permute-start(bf16[512,256]{1,0:T(8,128)(2,1)S(1)} %get-tuple-element.37), channel_id=1, source_target_pairs={{8,0},{12,4},{16,8},{20,12},{24,16},{28,20},{9,1},{13,5},{17,9},{2... | collective-permute-start | bytes 786440 | tf_op jit(solution)/shard_map/ppermute | solution.py:195
  86.5 1.9 %collective-permute-start.15 = (bf16[512,256]{1,0:T(8,128)(2,1)S(1)}, bf16[512,256]{1,0:T(8,128)(2,1)S(1)}, u32[]{:S(2)}, u32[]{:S(2)}) collective-permute-start(bf16[512,256]{1,0:T(8,128)(2,1)S(1)} %get-tuple-element.38), channel_id=1, source_target_pairs={{12,0},{16,4},{20,8},{24,12},{28,16},{13,1},{17,5},{21,9},{25,13},... | collective-permute-start | bytes 786440 | tf_op jit(solution)/shard_map/ppermute | solution.py:195
  90.7 31.9 %attend1.1 = (bf16[512,2048]{1,0:T(8,128)(2,1)}, bf16[512,2048]{1,0:T(8,128)(2,1)}, bf16[2560,256]{1,0:T(8,128)(2,1)}) custom-call(s32[2]{0:T(128)} %and_select_fusion.refs_0_, bf16[512,2048]{1,0:T(8,128)(2,1)} %refs_1_.3, bf16[512,2048]{1,0:T(8,128)(2,1)} %refs_2_.3, ...), custom_call_target="tpu_custom_call", output_to_operand_aliasing={{0}: (3, {}), {1}: (4, {})} | custom-call | flops 40000000000 | bytes 10000000 | tf_op jit(solution)/shard_map/attend1/pallas_call | solution.py:165
  123.7 15.0 %collective-permute-start.19 = (bf16[512,256]{1,0:T(8,128)(2,1)S(1)}, bf16[512,256]{1,0:T(8,128)(2,1)S(1)}, u32[]{:S(2)}, u32[]{:S(2)}) collective-permute-start(bf16[512,256]{1,0:T(8,128)(2,1)S(1)} %get-tuple-element.35), channel_id=1, source_target_pairs={{0,4},{4,0},{8,12},{12,8},{16,20},{20,16},{24,28},{28,24},{1,5},{5... | collective-permute-start | bytes 786440 | tf_op jit(solution)/shard_map/ppermute | solution.py:199
  138.8 6.2 %collective-permute-done.19 = bf16[512,256]{1,0:T(8,128)(2,1)S(1)} collective-permute-done((bf16[512,256]{1,0:T(8,128)(2,1)S(1)}, bf16[512,256]{1,0:T(8,128)(2,1)S(1)}, u32[]{:S(2)}, u32[]{:S(2)}) %collective-permute-start.19) | collective-permute-done | bytes 262176 | tf_op jit(solution)/shard_map/ppermute | solution.py:199
  146.0 1.9 %collective-permute-start.20 = (bf16[512,256]{1,0:T(8,128)(2,1)S(1)}, bf16[512,256]{1,0:T(8,128)(2,1)S(1)}, u32[]{:S(2)}, u32[]{:S(2)}) collective-permute-start(bf16[512,256]{1,0:T(8,128)(2,1)S(1)} %fusion.7), channel_id=1, source_target_pairs={{8,0},{12,4},{16,8},{20,12},{24,16},{28,20},{9,1},{13,5},{17,9},{2... | collective-permute-start | bytes 786440 | tf_op jit(solution)/shard_map/ppermute | solution.py:195
  148.0 7.3 %collective-permute-done.20 = bf16[512,256]{1,0:T(8,128)(2,1)S(1)} collective-permute-done((bf16[512,256]{1,0:T(8,128)(2,1)S(1)}, bf16[512,256]{1,0:T(8,128)(2,1)S(1)}, u32[]{:S(2)}, u32[]{:S(2)}) %collective-permute-start.20) | collective-permute-done | bytes 262176 | tf_op jit(solution)/shard_map/ppermute | solution.py:195
  156.4 1.9 %collective-permute-start.21 = (bf16[512,256]{1,0:T(8,128)(2,1)S(1)}, bf16[512,256]{1,0:T(8,128)(2,1)S(1)}, u32[]{:S(2)}, u32[]{:S(2)}) collective-permute-start(bf16[512,256]{1,0:T(8,128)(2,1)S(1)} %fusion.5), channel_id=1, source_target_pairs={{8,0},{12,4},{16,8},{20,12},{24,16},{28,20},{9,1},{13,5},{17,9},{2... | collective-permute-start | bytes 786440 | tf_op jit(solution)/shard_map/ppermute | solution.py:195
  159.5 5.2 %collective-permute-done.21 = bf16[512,256]{1,0:T(8,128)(2,1)S(1)} collective-permute-done((bf16[512,256]{1,0:T(8,128)(2,1)S(1)}, bf16[512,256]{1,0:T(8,128)(2,1)S(1)}, u32[]{:S(2)}, u32[]{:S(2)}) %collective-permute-start.21) | collective-permute-done | bytes 262176 | tf_op jit(solution)/shard_map/ppermute | solution.py:195
  (74 shorter events, 21.4 us)
Async XLA Ops:
  0.6 4.8 %collective-permute-start.1 = (s32[1,128]{1,0:T(1,128)}, s32[1,128]{1,0:T(1,128)S(1)}, u32[]{:S(2)}, u32[]{:S(2)}) collective-permute-start(s32[1,128]{1,0:T(1,128)} %bitcast.6), channel_id=1, source_target_pairs={{0,1},{1,0},{2,3},{3,2},{4,5},{5,4},{6,7},{7,6},{8,9},{9,8},{10,11... | collective-permute-start | bytes 1544 | tf_op jit(solution)/shard_map/ppermute | solution.py:211
  1.9 46.8 %copy-start.2 = (bf16[512,256]{1,0:T(8,128)(2,1)}, bf16[512,256]{1,0:T(8,128)(2,1)S(1)}, u32[]{:S(2)}) copy-start(bf16[512,256]{1,0:T(8,128)(2,1)S(1)} %pad_maximum_fusion.refs_7_) | copy-start | bytes 786436
  1.9 16.8 %collective-permute-start = (bf16[512,256]{1,0:T(8,128)(2,1)S(1)}, bf16[512,256]{1,0:T(8,128)(2,1)S(1)}, u32[]{:S(2)}, u32[]{:S(2)}) collective-permute-start(bf16[512,256]{1,0:T(8,128)(2,1)S(1)} %pad_maximum_fusion.refs_7_), channel_id=1, source_target_pairs={{0,8},{4,12},{8,16},{12,20},{16,24},{20,28},{1,9},{5,13},{9,17},{1... | collective-permute-start | bytes 786440 | tf_op jit(solution)/shard_map/ppermute | solution.py:195
  6.2 3.6 %collective-permute-start.2 = (s32[2,128]{1,0:T(2,128)S(1)}, s32[2,128]{1,0:T(2,128)S(1)}, u32[]{:S(2)}, u32[]{:S(2)}) collective-permute-start(s32[2,128]{1,0:T(2,128)S(1)} %add_select_fusion.1), channel_id=1, source_target_pairs={{0,2},{1,3},{2,0},{3,1},{4,6},{5,7},{6,4},{7,5},{8,10},{9,11},{10,... | collective-permute-start | bytes 3080 | tf_op jit(solution)/shard_map/ppermute | solution.py:211
  9.7 8.6 %collective-permute-start.7 = (s32[512]{0:T(512)S(1)}, s32[512]{0:T(512)S(1)}, u32[]{:S(2)}, u32[]{:S(2)}) collective-permute-start(s32[512]{0:T(512)S(1)} %fusion.8), channel_id=1, source_target_pairs={{0,4},{4,8},{8,12},{12,16},{16,20},{20,24},{24,28},{1,5},{5,9},{9,... | collective-permute-start | bytes 6152 | tf_op jit(solution)/shard_map/ppermute | solution.py:195
  13.2 68.2 %copy-start.3 = (bf16[512,256]{1,0:T(8,128)(2,1)}, bf16[512,256]{1,0:T(8,128)(2,1)S(1)}, u32[]{:S(2)}) copy-start(bf16[512,256]{1,0:T(8,128)(2,1)S(1)} %pad_maximum_fusion.1.refs_9_) | copy-start | bytes 786436
  13.2 5.5 %collective-permute-start.6 = (s32[512]{0:T(512)S(1)}, s32[512]{0:T(512)S(1)}, u32[]{:S(2)}, u32[]{:S(2)}) collective-permute-start(s32[512]{0:T(512)S(1)} %fusion.8), channel_id=1, source_target_pairs={{0,8},{4,12},{8,16},{12,20},{16,24},{20,28},{1,9},{5,13},{9,17},{1... | collective-permute-start | bytes 6152 | tf_op jit(solution)/shard_map/ppermute | solution.py:195
  15.1 7.4 %collective-permute-start.5 = (s32[512]{0:T(512)S(1)}, s32[512]{0:T(512)S(1)}, u32[]{:S(2)}, u32[]{:S(2)}) collective-permute-start(s32[512]{0:T(512)S(1)} %fusion.8), channel_id=1, source_target_pairs={{0,12},{4,16},{8,20},{12,24},{16,28},{1,13},{5,17},{9,21},{13,25},... | collective-permute-start | bytes 6152 | tf_op jit(solution)/shard_map/ppermute | solution.py:195
  17.1 6.5 %collective-permute-start.4 = (s32[512]{0:T(512)S(1)}, s32[512]{0:T(512)S(1)}, u32[]{:S(2)}, u32[]{:S(2)}) collective-permute-start(s32[512]{0:T(512)S(1)} %fusion.8), channel_id=1, source_target_pairs={{0,16},{4,20},{8,24},{12,28},{1,17},{5,21},{9,25},{13,29},{2,18},{... | collective-permute-start | bytes 6152 | tf_op jit(solution)/shard_map/ppermute | solution.py:195
  18.7 8.9 %collective-permute-start.3 = (bf16[512,256]{1,0:T(8,128)(2,1)S(1)}, bf16[512,256]{1,0:T(8,128)(2,1)S(1)}, u32[]{:S(2)}, u32[]{:S(2)}) collective-permute-start(bf16[512,256]{1,0:T(8,128)(2,1)S(1)} %collective-permute-done.refs_5_), channel_id=1, source_target_pairs={{0,8},{4,12},{8,16},{12,20},{16,24},{20,28},{1,9},{5,13},{9,17},{1... | collective-permute-start | bytes 786440 | tf_op jit(solution)/shard_map/ppermute | solution.py:195
  29.0 19.6 %collective-permute-start.9 = (bf16[512,256]{1,0:T(8,128)(2,1)S(1)}, bf16[512,256]{1,0:T(8,128)(2,1)S(1)}, u32[]{:S(2)}, u32[]{:S(2)}) collective-permute-start(bf16[512,256]{1,0:T(8,128)(2,1)S(1)} %get-tuple-element.50), channel_id=1, source_target_pairs={{0,4},{4,0},{8,12},{12,8},{16,20},{20,16},{24,28},{28,24},{1,5},{5... | collective-permute-start | bytes 786440 | tf_op jit(solution)/shard_map/ppermute | solution.py:199
  29.4 11.4 %collective-permute-start.8 = (bf16[512,256]{1,0:T(8,128)(2,1)S(1)}, bf16[512,256]{1,0:T(8,128)(2,1)S(1)}, u32[]{:S(2)}, u32[]{:S(2)}) collective-permute-start(bf16[512,256]{1,0:T(8,128)(2,1)S(1)} %get-tuple-element.51), channel_id=1, source_target_pairs={{0,4},{4,0},{8,12},{12,8},{16,20},{20,16},{24,28},{28,24},{1,5},{5... | collective-permute-start | bytes 786440 | tf_op jit(solution)/shard_map/ppermute | solution.py:199
  31.1 9.7 %collective-permute-start.10 = (bf16[512,256]{1,0:T(8,128)(2,1)S(1)}, bf16[512,256]{1,0:T(8,128)(2,1)S(1)}, u32[]{:S(2)}, u32[]{:S(2)}) collective-permute-start(bf16[512,256]{1,0:T(8,128)(2,1)S(1)} %pad_maximum_fusion.1.refs_9_), channel_id=1, source_target_pairs={{0,8},{4,12},{8,16},{12,20},{16,24},{20,28},{1,9},{5,13},{9,17},{1... | collective-permute-start | bytes 786440 | tf_op jit(solution)/shard_map/ppermute | solution.py:195
  40.8 47.6 %collective-permute-start.12 = (bf16[512,256]{1,0:T(8,128)(2,1)S(1)}, bf16[512,256]{1,0:T(8,128)(2,1)S(1)}, u32[]{:S(2)}, u32[]{:S(2)}) collective-permute-start(bf16[512,256]{1,0:T(8,128)(2,1)S(1)} %collective-permute-done.10.refs_7_), channel_id=1, source_target_pairs={{0,4},{4,8},{8,12},{12,16},{16,20},{20,24},{24,28},{1,5},{5,9},{9,... | collective-permute-start | bytes 786440 | tf_op jit(solution)/shard_map/ppermute | solution.py:195
  43.4 46.6 %collective-permute-start.11 = (bf16[512,256]{1,0:T(8,128)(2,1)S(1)}, bf16[512,256]{1,0:T(8,128)(2,1)S(1)}, u32[]{:S(2)}, u32[]{:S(2)}) collective-permute-start(bf16[512,256]{1,0:T(8,128)(2,1)S(1)} %collective-permute-done.10.refs_7_), channel_id=1, source_target_pairs={{0,8},{4,12},{8,16},{12,20},{16,24},{20,28},{1,9},{5,13},{9,17},{1... | collective-permute-start | bytes 786440 | tf_op jit(solution)/shard_map/ppermute | solution.py:195
  45.5 41.0 %collective-permute-start.13 = (bf16[512,256]{1,0:T(8,128)(2,1)S(1)}, bf16[512,256]{1,0:T(8,128)(2,1)S(1)}, u32[]{:S(2)}, u32[]{:S(2)}) collective-permute-start(bf16[512,256]{1,0:T(8,128)(2,1)S(1)} %pad_maximum_fusion.1.refs_9_), channel_id=1, source_target_pairs={{0,4},{4,8},{8,12},{12,16},{16,20},{20,24},{24,28},{1,5},{5,9},{9,... | collective-permute-start | bytes 786440 | tf_op jit(solution)/shard_map/ppermute | solution.py:195
  82.6 41.0 %collective-permute-start.17 = (bf16[512,256]{1,0:T(8,128)(2,1)S(1)}, bf16[512,256]{1,0:T(8,128)(2,1)S(1)}, u32[]{:S(2)}, u32[]{:S(2)}) collective-permute-start(bf16[512,256]{1,0:T(8,128)(2,1)S(1)} %get-tuple-element.36), channel_id=1, source_target_pairs={{4,0},{8,4},{12,8},{16,12},{20,16},{24,20},{28,24},{5,1},{9,5},{13... | collective-permute-start | bytes 786440 | tf_op jit(solution)/shard_map/ppermute | solution.py:195
  84.6 39.1 %collective-permute-start.16 = (bf16[512,256]{1,0:T(8,128)(2,1)S(1)}, bf16[512,256]{1,0:T(8,128)(2,1)S(1)}, u32[]{:S(2)}, u32[]{:S(2)}) collective-permute-start(bf16[512,256]{1,0:T(8,128)(2,1)S(1)} %get-tuple-element.37), channel_id=1, source_target_pairs={{8,0},{12,4},{16,8},{20,12},{24,16},{28,20},{9,1},{13,5},{17,9},{2... | collective-permute-start | bytes 786440 | tf_op jit(solution)/shard_map/ppermute | solution.py:195
  86.5 37.1 %collective-permute-start.15 = (bf16[512,256]{1,0:T(8,128)(2,1)S(1)}, bf16[512,256]{1,0:T(8,128)(2,1)S(1)}, u32[]{:S(2)}, u32[]{:S(2)}) collective-permute-start(bf16[512,256]{1,0:T(8,128)(2,1)S(1)} %get-tuple-element.38), channel_id=1, source_target_pairs={{12,0},{16,4},{20,8},{24,12},{28,16},{13,1},{17,5},{21,9},{25,13},... | collective-permute-start | bytes 786440 | tf_op jit(solution)/shard_map/ppermute | solution.py:195
  88.5 35.2 %collective-permute-start.14 = (bf16[512,256]{1,0:T(8,128)(2,1)S(1)}, bf16[512,256]{1,0:T(8,128)(2,1)S(1)}, u32[]{:S(2)}, u32[]{:S(2)}) collective-permute-start(bf16[512,256]{1,0:T(8,128)(2,1)S(1)} %get-tuple-element.39), channel_id=1, source_target_pairs={{16,0},{20,4},{24,8},{28,12},{17,1},{21,5},{25,9},{29,13},{18,2},{... | collective-permute-start | bytes 786440 | tf_op jit(solution)/shard_map/ppermute | solution.py:195
  123.7 21.3 %collective-permute-start.19 = (bf16[512,256]{1,0:T(8,128)(2,1)S(1)}, bf16[512,256]{1,0:T(8,128)(2,1)S(1)}, u32[]{:S(2)}, u32[]{:S(2)}) collective-permute-start(bf16[512,256]{1,0:T(8,128)(2,1)S(1)} %get-tuple-element.35), channel_id=1, source_target_pairs={{0,4},{4,0},{8,12},{12,8},{16,20},{20,16},{24,28},{28,24},{1,5},{5... | collective-permute-start | bytes 786440 | tf_op jit(solution)/shard_map/ppermute | solution.py:199
  138.7 9.2 %collective-permute-start.18 = (bf16[512,256]{1,0:T(8,128)(2,1)S(1)}, bf16[512,256]{1,0:T(8,128)(2,1)S(1)}, u32[]{:S(2)}, u32[]{:S(2)}) collective-permute-start(bf16[512,256]{1,0:T(8,128)(2,1)S(1)} %get-tuple-element.41), channel_id=1, source_target_pairs={{0,4},{4,0},{8,12},{12,8},{16,20},{20,16},{24,28},{28,24},{1,5},{5... | collective-permute-start | bytes 786440 | tf_op jit(solution)/shard_map/ppermute | solution.py:199
  146.0 9.3 %collective-permute-start.20 = (bf16[512,256]{1,0:T(8,128)(2,1)S(1)}, bf16[512,256]{1,0:T(8,128)(2,1)S(1)}, u32[]{:S(2)}, u32[]{:S(2)}) collective-permute-start(bf16[512,256]{1,0:T(8,128)(2,1)S(1)} %fusion.7), channel_id=1, source_target_pairs={{8,0},{12,4},{16,8},{20,12},{24,16},{28,20},{9,1},{13,5},{17,9},{2... | collective-permute-start | bytes 786440 | tf_op jit(solution)/shard_map/ppermute | solution.py:195
  156.4 8.3 %collective-permute-start.21 = (bf16[512,256]{1,0:T(8,128)(2,1)S(1)}, bf16[512,256]{1,0:T(8,128)(2,1)S(1)}, u32[]{:S(2)}, u32[]{:S(2)}) collective-permute-start(bf16[512,256]{1,0:T(8,128)(2,1)S(1)} %fusion.5), channel_id=1, source_target_pairs={{8,0},{12,4},{16,8},{20,12},{24,16},{28,20},{9,1},{13,5},{17,9},{2... | collective-permute-start | bytes 786440 | tf_op jit(solution)/shard_map/ppermute | solution.py:195
  (9 other events, 125.6 us)
where the time goes:
time: 168 us; the launch traced here: 167 us
  Pallas kernels  63.9 us (38%)
  starting transfers between devices  53.8 us (32%)
  waiting for transfers between devices  34.9 us (21%)
  other arithmetic  8.49 us (5%)
  local copies, waits for them, and re-layouts  5 us (3%)
    pallas_call x2, Pallas kernels, attend(): pl.pallas_call(kernel, grid_spec=pltpu.PrefetchScalarGridSpec(num_scalar_...  63.9 us
    ppermute x16, starting transfers between devices, hop(): lax.ppermute(x, 'ctx', [(s, s + shift) for s in range(count) if 0 <= s +...  35 us
    ppermute x16, waiting for transfers between devices, hop(): lax.ppermute(x, 'ctx', [(s, s + shift) for s in range(count) if 0 <= s +...  19.8 us
    ppermute x4, starting transfers between devices, swap(): lax.ppermute(x, 'ctx', [(s, s ^ 1) for s in range(lax.axis_size('ctx'))])  17.2 us
    ppermute x4, waiting for transfers between devices, swap(): lax.ppermute(x, 'ctx', [(s, s ^ 1) for s in range(lax.axis_size('ctx'))])  13 us
  transfers between devices with their start and end apart: 22, of which 9 were waited for; matrix products, arithmetic and copies ran while one was open for 4% of the time, Pallas kernels for 38%

commit v1 on v0

v1 whole, which is shorter than its diff:
```python
import functools, math
import jax, jax.numpy as jnp
from jax import lax
from jax.sharding import PartitionSpec as P
from jax.experimental import pallas as pl
from jax.experimental.pallas import tpu as pltpu

HD = 128
KB = 256
WIDTHS = (4, 2, 1)
NEG = -1e30
BIG = 1e30
F32, BF16 = jnp.float32, jnp.bfloat16


def dot(a, b):
    return lax.dot_general(a, b, (((1,), (0,)), ((), ())), preferred_element_type=F32)


def body(group, nkeys, lo_ref, q_ref, g_ref, kv_refs, start_ref, o_ref, dq_ref, dkv_refs,
         k_s, v_s, kt_s, vt_s, qt_s, gt_s, qs_s, gs_s, s_s, u_s, bias_s, db_s, ot_s, dqt_s, m_s, dk_s, dv_s):
    r = pl.program_id(0)
    rb = q_ref.shape[0]
    nb = nkeys // KB
    slab = kv_refs[0].shape[0]
    per = slab // KB
    c2 = math.log2(math.e) / math.sqrt(HD)

    @pl.when(r == 0)
    def _():
        for n, ref in enumerate(kv_refs):
            for t in range(per):
                at = slice((n * per + t) * KB, (n * per + t + 1) * KB)

                @pl.when(n * per + t >= lo_ref[0])
                def _():
                    k = ref[t * KB:(t + 1) * KB, :HD]
                    v = ref[t * KB:(t + 1) * KB, HD:]
                    k_s[at, :] = k
                    v_s[at, :] = v
                    kt_s[:, at] = k.T
                    vt_s[:HD, at] = v.T
        vt_s[HD:, :] = jnp.ones((vt_s.shape[0] - HD, nkeys), BF16)
        dk_s[...] = jnp.zeros_like(dk_s)
        dv_s[...] = jnp.zeros_like(dv_s)

    for h in range(group):
        q = q_ref[:, h * HD:(h + 1) * HD]
        g = g_ref[:, h * HD:(h + 1) * HD]
        qs_s[h * rb:(h + 1) * rb, :] = q
        qt_s[:, h * rb:(h + 1) * rb] = q.T
        gt_s[:, h * rb:(h + 1) * rb] = g.T

    lo = lo_ref[r]
    hi = nb - pl.num_programs(0) * rb // KB + (r + 1) * rb // KB
    start = start_ref[0:1, :]
    qpos = (nkeys - pl.num_programs(0) * rb) + r * rb + lax.broadcasted_iota(jnp.int32, (1, rb), 1)
    dqt_s[...] = jnp.zeros_like(dqt_s)

    def span(j, wide):
        return pl.ds(pl.multiple_of(j * KB, KB), wide * KB)

    def set_bias(j, wide):
        kpos = j * KB + lax.broadcasted_iota(jnp.int32, (wide * KB, rb), 0)
        bias_s[:wide * KB, :] = jnp.where((kpos >= start) & (kpos <= qpos), BIG, NEG)

    def scores(j, wide, cols):
        return jnp.minimum(dot(k_s[span(j, wide), :], qt_s[:, cols]), bias_s[:wide * KB, :])

    def fold_max(s):
        return jnp.max(s.reshape(KB // 8, 8, rb), axis=0)

    def weigh(j, wide, s, cols):
        u_s[span(j, wide), cols] = jnp.exp2(s * c2 - m_s[0:1, cols]).astype(BF16)

    def attend_step(j, wide):
        set_bias(j, wide)
        for cols in heads:
            weigh(j, wide, scores(j, wide, cols), cols)
        ot_s[...] += dot(vt_s[:, span(j, wide)], u_s[span(j, wide), :])

    def grad_step(j, wide):
        at = span(j, wide)
        for h, cols in enumerate(heads):
            dp = dot(v_s[at, :], gt_s[:, cols])
            db_s[:wide * KB, cols] = (u_s[at, cols].astype(F32) * (dp - deltas[h])).astype(BF16)
        db = db_s[:wide * KB, :]
        dqt_s[...] += dot(kt_s[:, at], db)
        dk_s[at, :] += dot(db, qs_s[...])
        dv_s[at, :] += dot(u_s[at, :], gs_s[...])

    def blocks(first, end, step):
        left = end - first
        for n, wide in enumerate(WIDTHS):
            if n == 0:
                count = left // wide

                @pl.loop(0, count)
                def _(i):
                    step(first + i * wide, wide)

                first, left = first + count * wide, left - count * wide
            else:
                take = left >= wide

                @pl.when(take)
                def _(first=first):
                    step(first, wide)

                first, left = first + jnp.where(take, wide, 0), left - jnp.where(take, wide, 0)

    heads = [slice(h * rb, (h + 1) * rb) for h in range(group)]

    last = hi - 1
    set_bias(last, 1)
    for cols in heads:
        s = scores(last, 1, cols)
        s_s[:, cols] = s
        m_s[0:1, cols] = jnp.max(fold_max(s), axis=0, keepdims=True) * c2
    for cols in heads:
        weigh(last, 1, s_s[:, cols], cols)
    ot_s[...] = dot(vt_s[:, span(last, 1)], u_s[span(last, 1), :])
    blocks(lo, last, attend_step)

    @pl.when(jnp.logical_not(jnp.max(ot_s[HD:HD + 1, :]) < 2.0 ** 60))
    def _():
        m_s[...] = jnp.full_like(m_s, NEG)

        def each_head(step):
            @pl.loop(lo, hi)
            def _(j):
                set_bias(j, 1)

                @pl.loop(0, group)
                def _(h):
                    step(j, pl.ds(pl.multiple_of(h * rb, rb), rb))

        def raise_max(j, cols):
            m_s[:, cols] = jnp.maximum(m_s[:, cols], fold_max(scores(j, 1, cols)))

        def redo(j, cols):
            weigh(j, 1, scores(j, 1, cols), cols)
            ot_s[:, cols] += dot(vt_s[:, span(j, 1)], u_s[span(j, 1), cols])

        each_head(raise_max)
        m_s[0:1, :] = jnp.max(m_s[...], axis=0, keepdims=True) * c2
        ot_s[...] = jnp.zeros_like(ot_s)
        each_head(redo)

    rl = 1.0 / ot_s[HD:HD + 1, :]
    deltas = []
    for h in range(group):
        cols = slice(h * rb, (h + 1) * rb)
        ob = (ot_s[:HD, cols] * rl[:, cols]).astype(BF16)
        o_ref[:, h * HD:(h + 1) * HD] = ob.T
        gt = gt_s[:, cols].astype(F32) * rl[:, cols]
        deltas.append(jnp.sum(ob.astype(F32) * gt, axis=0, keepdims=True))
        gt = gt.astype(BF16)
        gt_s[:, cols] = gt
        gs_s[h * rb:(h + 1) * rb, :] = gt.T

    blocks(lo, hi, grad_step)

    scale = 1.0 / math.sqrt(HD)
    for h in range(group):
        cols = slice(h * rb, (h + 1) * rb)
        dq_ref[:, h * HD:(h + 1) * HD] = (dqt_s[:, cols] * scale).astype(BF16).T

    @pl.when(r == pl.num_programs(0) - 1)
    def _():
        for n, ref in enumerate(dkv_refs):
            at = slice(n * slab, (n + 1) * slab)
            ref[:, :HD] = (dk_s[at, :] * scale).astype(BF16)
            ref[:, HD:] = dv_s[at, :].astype(BF16)


def attend(q, g, kvs, start, lo, chunk, group, prev=None, rb=256):
    rows, width = q.shape
    gw = group * HD
    slab = kvs[0].shape[0]
    nkeys = slab * len(kvs)
    R = group * rb
    n = len(kvs)

    def kernel(*refs):
        if prev is None:
            lo_ref, q_ref, g_ref, *rest = refs
        else:
            lo_ref, q_ref, g_ref, _, _, *rest = refs
        kv_refs, rest = rest[:n], rest[n:]
        start_ref, o_ref, dq_ref, *rest = rest
        body(group, nkeys, lo_ref, q_ref, g_ref, kv_refs, start_ref, o_ref, dq_ref, rest[:n], *rest[n:])

    blk = pl.BlockSpec((rb, gw), lambda r, lo: (r, chunk))
    extra = [] if prev is None else list(prev)
    return pl.pallas_call(
        kernel,
        grid_spec=pltpu.PrefetchScalarGridSpec(
            num_scalar_prefetch=1,
            grid=(rows // rb,),
            in_specs=[blk, blk] + [pl.BlockSpec(memory_space=pl.ANY)] * len(extra)
            + [pl.BlockSpec((slab, 2 * HD), lambda r, lo: (0, 0))] * n
            + [pl.BlockSpec((1, rb), lambda r, lo: (0, r))],
            out_specs=[blk, blk] + [pl.BlockSpec((slab, 2 * HD), lambda r, lo: (0, 0))] * n,
            scratch_shapes=[
                pltpu.VMEM((nkeys, HD), BF16), pltpu.VMEM((nkeys, HD), BF16),
                pltpu.VMEM((HD, nkeys), BF16), pltpu.VMEM((HD + 16, nkeys), BF16),
                pltpu.VMEM((HD, R), BF16), pltpu.VMEM((HD, R), BF16),
                pltpu.VMEM((R, HD), BF16), pltpu.VMEM((R, HD), BF16),
                pltpu.VMEM((KB, R), F32), pltpu.VMEM((nkeys, R), BF16),
                pltpu.VMEM((WIDTHS[0] * KB, rb), F32), pltpu.VMEM((WIDTHS[0] * KB, R), BF16),
                pltpu.VMEM((HD + 16, R), F32), pltpu.VMEM((HD, R), F32),
                pltpu.VMEM((8, R), F32),
                pltpu.VMEM((nkeys, HD), F32), pltpu.VMEM((nkeys, HD), F32),
            ],
        ),
        out_shape=[jax.ShapeDtypeStruct((rows, width), BF16), jax.ShapeDtypeStruct((rows, width), BF16),
                   *[jax.ShapeDtypeStruct((slab, 2 * HD), BF16)] * n],
        input_output_aliases={} if prev is None else {3: 0, 4: 1},
        compiler_params=pltpu.CompilerParams(vmem_limit_bytes=56 * 1024 * 1024),
        name=f"attend{chunk}",
        cost_estimate=pl.CostEstimate(flops=40_000_000_000, bytes_accessed=10_000_000, transcendentals=0),
    )(lo, q, g, *extra, *kvs, start)
def hop(x, shift):
    count = lax.axis_size("ctx")
    return lax.ppermute(x, "ctx", [(s, s + shift) for s in range(count) if 0 <= s + shift < count])


def swap(x):
    return lax.ppermute(x, "ctx", [(s, s ^ 1) for s in range(lax.axis_size("ctx"))])


def after(x, *others):
    return lax.optimization_barrier((x, *others))[0]


def gather_ids(doc_ids):
    tps = lax.axis_size("tp")
    ids = doc_ids[None]
    step = 1
    while step < tps:
        other = lax.ppermute(ids, "tp", [(t, t ^ step) for t in range(tps)])
        low = (lax.axis_index("tp") // step) % 2 == 0
        ids = jnp.where(low, jnp.concatenate([ids, other]), jnp.concatenate([other, ids]))
        step *= 2
    return ids.reshape(-1)


def on_device(queries, keys, values, grad_out, doc_ids):
    slab, width = keys.shape
    chunks = width // HD
    group = queries.shape[1] // width
    me = lax.axis_index("ctx")
    odd = lax.rem(me, 2) == 1
    rb = 256

    def own_part(c):
        return jnp.concatenate([keys[:, c * HD:(c + 1) * HD], values[:, c * HD:(c + 1) * HD]], axis=1)

    own = [own_part(c) for c in range(chunks)]
    two = after(hop(own[0], 2))
    ids = gather_ids(doc_ids)
    earlier = [jnp.where(me >= back, hop(ids, back), -1) for back in (4, 3, 2, 1)]
    four = hop(two, 2)
    one = swap(jnp.where(odd, two, own[0]))
    four, one, earlier, own[1:] = lax.optimization_barrier((four, one, earlier, own[1:]))
    three = swap(jnp.where(odd, four, two))
    ahead = [hop(x, 2) for x in own[1:2]]
    three, ahead, own[1:2] = lax.optimization_barrier((three, ahead, own[1:2]))
    context = jnp.concatenate(earlier + [ids])
    start = jnp.sum((context[:, None] < ids[None, :]).astype(jnp.int32), axis=0)
    lo = start.reshape(slab // rb, rb)[:, 0] // KB
    start = start[None]
    blocks = [four, three, two, one, own[0]]

    outs = None
    grads = []
    for c in range(chunks):
        following = None
        if c + 1 < chunks:
            mine, theirs = own[c + 1], ahead[c] if c < len(ahead) else hop(own[c + 1], 2)
            following = [hop(theirs, 2), hop(theirs, 1), theirs, hop(mine, 1), mine]
        att, gq, *parts = attend(queries, grad_out, blocks, start, lo, c, group, outs, rb)
        outs = (att, gq)
        four_grad, three_grad, two_grad, one_grad, own_grad = parts
        if following is not None:
            back = [hop(four_grad, -4), hop(three_grad, -3), hop(two_grad, -2), hop(one_grad, -1)]
            grads.append([own_grad] + back)
        else:
            f32 = lambda x: x.astype(F32)
            zero = jnp.zeros((slab, 2 * HD), F32)
            swap3 = swap(after(three_grad, *(x for part in grads for x in part)))
            swap1 = f32(swap(after(one_grad, swap3)))
            swap3 = f32(swap3)
            four_grad = (f32(four_grad) + jnp.where(odd, swap3, zero)).astype(BF16)
            two_grad = f32(two_grad) + jnp.where(odd, swap1, swap3)
            two_grad = (two_grad + f32(hop(four_grad, -2))).astype(BF16)
            grads.append([f32(own_grad) + jnp.where(odd, zero, swap1), hop(two_grad, -2)])
        blocks = following
    sums = [sum(x.astype(F32) for x in parts) for parts in grads]
    grad_k = jnp.concatenate([x[:, :HD] for x in sums], axis=1).astype(BF16)
    grad_v = jnp.concatenate([x[:, HD:] for x in sums], axis=1).astype(BF16)
    return outs[0], outs[1], grad_k, grad_v


def solution(mesh):
    return jax.shard_map(
        on_device,
        mesh=mesh,
        in_specs=(P("ctx", "tp"), P("ctx", "tp"), P("ctx", "tp"), P("ctx", "tp"), P(("ctx", "tp"))),
        out_specs=(P("ctx", "tp"), P("ctx", "tp"), P("ctx", "tp"), P("ctx", "tp")),
        check_vma=False,
    )
```

time: 168 us -> 149 us (0.89)
  Pallas kernels: 63.9 us -> 32 us
  waiting for transfers between devices: 34.9 us -> 60.3 us
  starting transfers between devices: 53.8 us -> 46.7 us
  local copies, waits for them, and re-layouts: 5 us -> 2.05 us
  other arithmetic: 8.49 us -> 6.57 us
    pallas_call x2, Pallas kernels: 63.9 us -> 32 us  [attend(): pl.pallas_call(kernel, grid_spec=pltpu.PrefetchScalarGridSpec(num_scalar_...]
    ppermute x16, waiting for transfers between devices: 19.8 us -> 42.5 us  [hop(): lax.ppermute(x, 'ctx', [(s, s + shift) for s in range(count) if 0 <= s +...]
    ppermute x4, starting transfers between devices: 17.2 us -> 6.19 us  [swap(): lax.ppermute(x, 'ctx', [(s, s ^ 1) for s in range(lax.axis_size('ctx'))])]
    ppermute x16, starting transfers between devices: 35 us -> 38.9 us  [hop(): lax.ppermute(x, 'ctx', [(s, s + shift) for s in range(count) if 0 <= s +...]
    ppermute x4, waiting for transfers between devices: 13 us -> 15.8 us  [swap(): lax.ppermute(x, 'ctx', [(s, s ^ 1) for s in range(lax.axis_size('ctx'))])]
    another operation x2 -> x0, local copies, waits for them, and re-layouts: 2.32 us -> none  [on_device(): four, three, two, one, own_grad = parts.reshape(5, slab, 2 * HD)]
    another operation x2, other arithmetic: 2.18 us -> 0.28 us
  transfers between devices with their start and end apart: 22 -> 22, of which waited for: 9 -> 14; matrix products, arithmetic and copies ran while one was open for 4% -> 3% of each run, Pallas kernels for 38% -> 22%
where the time goes in v1:
time: 149 us
  waiting for transfers between devices  60.3 us (40%)
  starting transfers between devices  46.7 us (31%)
  Pallas kernels  32 us (21%)
  other arithmetic  6.57 us (4%)
  local copies, waits for them, and re-layouts  2.05 us (1%)
    ppermute x16, waiting for transfers between devices, hop(): lax.ppermute(x, 'ctx', [(s, s + shift) for s in range(count) if 0 <= s +...  42.5 us
    ppermute x16, starting transfers between devices, hop(): lax.ppermute(x, 'ctx', [(s, s + shift) for s in range(count) if 0 <= s +...  38.9 us
    pallas_call x2, Pallas kernels, attend(): pl.pallas_call(kernel, grid_spec=pltpu.PrefetchScalarGridSpec(num_scalar_...  32 us
    ppermute x4, waiting for transfers between devices, swap(): lax.ppermute(x, 'ctx', [(s, s ^ 1) for s in range(lax.axis_size('ctx'))])  15.8 us
    ppermute x4, starting transfers between devices, swap(): lax.ppermute(x, 'ctx', [(s, s ^ 1) for s in range(lax.axis_size('ctx'))])  6.19 us
  transfers between devices with their start and end apart: 22, of which 14 were waited for; matrix products, arithmetic and copies ran while one was open for 3% of the time, Pallas kernels for 22%

profile of v1, /device:TPU:16, one launch (start us, length us, event | category | flops | bytes accessed | tf_op | source)
XLA Modules:
  0.0 148.8 jit_solution(8530657737897192333)
XLA Ops:
  1.9 3.5 %collective-permute-start = (bf16[512,256]{1,0:T(8,128)(2,1)S(1)}, bf16[512,256]{1,0:T(8,128)(2,1)S(1)}, u32[]{:S(2)}, u32[]{:S(2)}) collective-permute-start(bf16[512,256]{1,0:T(8,128)(2,1)S(1)} %pad_maximum_fusion.refs_7_), channel_id=1, source_target_pairs={{0,8},{4,12},{8,16},{12,20},{16,24},{20,28},{1,9},{5,13},{9,17},{1... | collective-permute-start | bytes 786440 | tf_op jit(solution)/shard_map/ppermute | solution.py:226
  7.7 2.0 %collective-permute-done.4 = s32[2,128]{1,0:T(2,128)S(1)} collective-permute-done((s32[2,128]{1,0:T(2,128)S(1)}, s32[2,128]{1,0:T(2,128)S(1)}, u32[]{:S(2)}, u32[]{:S(2)}) %collective-permute-start.4) | collective-permute-done | bytes 1056 | tf_op jit(solution)/shard_map/ppermute | solution.py:242
  9.7 3.4 %collective-permute-start.8 = (s32[512]{0:T(512)S(1)}, s32[512]{0:T(512)S(1)}, u32[]{:S(2)}, u32[]{:S(2)}) collective-permute-start(s32[512]{0:T(512)S(1)} %fusion.8), channel_id=1, source_target_pairs={{0,4},{4,8},{8,12},{12,16},{16,20},{20,24},{24,28},{1,5},{5,9},{9,... | collective-permute-start | bytes 6152 | tf_op jit(solution)/shard_map/ppermute | solution.py:226
  13.2 1.9 %collective-permute-start.7 = (s32[512]{0:T(512)S(1)}, s32[512]{0:T(512)S(1)}, u32[]{:S(2)}, u32[]{:S(2)}) collective-permute-start(s32[512]{0:T(512)S(1)} %fusion.8), channel_id=1, source_target_pairs={{0,8},{4,12},{8,16},{12,20},{16,24},{20,28},{1,9},{5,13},{9,17},{1... | collective-permute-start | bytes 6152 | tf_op jit(solution)/shard_map/ppermute | solution.py:226
  15.1 1.9 %collective-permute-start.6 = (s32[512]{0:T(512)S(1)}, s32[512]{0:T(512)S(1)}, u32[]{:S(2)}, u32[]{:S(2)}) collective-permute-start(s32[512]{0:T(512)S(1)} %fusion.8), channel_id=1, source_target_pairs={{0,12},{4,16},{8,20},{12,24},{16,28},{1,13},{5,17},{9,21},{13,25},... | collective-permute-start | bytes 6152 | tf_op jit(solution)/shard_map/ppermute | solution.py:226
  18.7 1.9 %collective-permute-start.1 = (bf16[512,256]{1,0:T(8,128)(2,1)S(1)}, bf16[512,256]{1,0:T(8,128)(2,1)S(1)}, u32[]{:S(2)}, u32[]{:S(2)}) collective-permute-start(bf16[512,256]{1,0:T(8,128)(2,1)S(1)} %collective-permute-done.refs_5_), channel_id=1, source_target_pairs={{0,8},{4,12},{8,16},{12,20},{16,24},{20,28},{1,9},{5,13},{9,17},{1... | collective-permute-start | bytes 786440 | tf_op jit(solution)/shard_map/ppermute | solution.py:226
  23.6 4.3 %collective-permute-done.2.refs_6_ = bf16[512,256]{1,0:T(8,128)(2,1)S(1)} collective-permute-done((bf16[512,256]{1,0:T(8,128)(2,1)S(1)}, bf16[512,256]{1,0:T(8,128)(2,1)S(1)}, u32[]{:S(2)}, u32[]{:S(2)}) %collective-permute-start.2) | collective-permute-done | bytes 262176 | tf_op jit(solution)/shard_map/ppermute | solution.py:230
  32.0 3.6 %collective-permute-done.9.refs_4_ = bf16[512,256]{1,0:T(8,128)(2,1)S(1)} collective-permute-done((bf16[512,256]{1,0:T(8,128)(2,1)S(1)}, bf16[512,256]{1,0:T(8,128)(2,1)S(1)}, u32[]{:S(2)}, u32[]{:S(2)}) %collective-permute-start.9) | collective-permute-done | bytes 262176 | tf_op jit(solution)/shard_map/ppermute | solution.py:230
  35.6 2.1 %collective-permute-done.10.refs_7_ = bf16[512,256]{1,0:T(8,128)(2,1)S(1)} collective-permute-done((bf16[512,256]{1,0:T(8,128)(2,1)S(1)}, bf16[512,256]{1,0:T(8,128)(2,1)S(1)}, u32[]{:S(2)}, u32[]{:S(2)}) %collective-permute-start.10) | collective-permute-done | bytes 262176 | tf_op jit(solution)/shard_map/ppermute | solution.py:226
  37.7 3.7 %collective-permute-start.12 = (bf16[512,256]{1,0:T(8,128)(2,1)S(1)}, bf16[512,256]{1,0:T(8,128)(2,1)S(1)}, u32[]{:S(2)}, u32[]{:S(2)}) collective-permute-start(bf16[512,256]{1,0:T(8,128)(2,1)S(1)} %collective-permute-done.10.refs_7_), channel_id=1, source_target_pairs={{0,4},{4,8},{8,12},{12,16},{16,20},{20,24},{24,28},{1,5},{5,9},{9,... | collective-permute-start | bytes 786440 | tf_op jit(solution)/shard_map/ppermute | solution.py:226
  41.4 2.0 %collective-permute-start.11 = (bf16[512,256]{1,0:T(8,128)(2,1)S(1)}, bf16[512,256]{1,0:T(8,128)(2,1)S(1)}, u32[]{:S(2)}, u32[]{:S(2)}) collective-permute-start(bf16[512,256]{1,0:T(8,128)(2,1)S(1)} %collective-permute-done.10.refs_7_), channel_id=1, source_target_pairs={{0,8},{4,12},{8,16},{12,20},{16,24},{20,28},{1,9},{5,13},{9,17},{1... | collective-permute-start | bytes 786440 | tf_op jit(solution)/shard_map/ppermute | solution.py:226
  43.4 1.9 %collective-permute-start.13 = (bf16[512,256]{1,0:T(8,128)(2,1)S(1)}, bf16[512,256]{1,0:T(8,128)(2,1)S(1)}, u32[]{:S(2)}, u32[]{:S(2)}) collective-permute-start(bf16[512,256]{1,0:T(8,128)(2,1)S(1)} %pad_maximum_fusion.1.refs_9_), channel_id=1, source_target_pairs={{0,4},{4,8},{8,12},{12,16},{16,20},{20,24},{24,28},{1,5},{5,9},{9,... | collective-permute-start | bytes 786440 | tf_op jit(solution)/shard_map/ppermute | solution.py:226
  45.4 16.1 %attend0.1 = (bf16[512,2048]{1,0:T(8,128)(2,1)}, bf16[512,2048]{1,0:T(8,128)(2,1)}, bf16[512,256]{1,0:T(8,128)(2,1)}, bf16[512,256]{1,0:T(8,128)(2,1)}, bf16[512...) custom-call(s32[2]{0:T(128)} %and_select_fusion.refs_0_, bf16[512,2048]{1,0:T(8,128)(2,1)} %refs_1_.3, ...), custom_call_target="tpu_custom_call" | custom-call | flops 40000000000 | bytes 10000000 | tf_op jit(solution)/shard_map/attend0/pallas_call | solution.py:196
  63.0 6.0 %collective-permute-start.15 = (bf16[512,256]{1,0:T(8,128)(2,1)}, bf16[512,256]{1,0:T(8,128)(2,1)S(1)}, u32[]{:S(2)}, u32[]{:S(2)}) collective-permute-start(bf16[512,256]{1,0:T(8,128)(2,1)} %get-tuple-element.46), channel_id=1, source_target_pairs={{12,0},{16,4},{20,8},{24,12},{28,16},{13,1},{17,5},{21,9},{25,13},... | collective-permute-start | bytes 786440 | tf_op jit(solution)/shard_map/ppermute | solution.py:226
  71.0 2.2 %collective-permute-start.17 = (bf16[512,256]{1,0:T(8,128)(2,1)}, bf16[512,256]{1,0:T(8,128)(2,1)S(1)}, u32[]{:S(2)}, u32[]{:S(2)}) collective-permute-start(bf16[512,256]{1,0:T(8,128)(2,1)} %get-tuple-element.48), channel_id=1, source_target_pairs={{4,0},{8,4},{12,8},{16,12},{20,16},{24,20},{28,24},{5,1},{9,5},{13... | collective-permute-start | bytes 786440 | tf_op jit(solution)/shard_map/ppermute | solution.py:226
  73.9 16.0 %attend1.1 = (bf16[512,2048]{1,0:T(8,128)(2,1)}, bf16[512,2048]{1,0:T(8,128)(2,1)}, bf16[512,256]{1,0:T(8,128)(2,1)}, bf16[512,256]{1,0:T(8,128)(2,1)}, bf16[512...) custom-call(s32[2]{0:T(128)} %and_select_fusion.refs_0_, ...), custom_call_target="tpu_custom_call", output_to_operand_aliasing={{0}: (3, {}), {1}: (4, {})} | custom-call | flops 40000000000 | bytes 10000000 | tf_op jit(solution)/shard_map/attend1/pallas_call | solution.py:196
  89.9 2.3 %collective-permute-done.15 = bf16[512,256]{1,0:T(8,128)(2,1)S(1)} collective-permute-done((bf16[512,256]{1,0:T(8,128)(2,1)}, bf16[512,256]{1,0:T(8,128)(2,1)S(1)}, u32[]{:S(2)}, u32[]{:S(2)}) %collective-permute-start.15) | collective-permute-done | bytes 262176 | tf_op jit(solution)/shard_map/ppermute | solution.py:226
  92.7 2.5 %collective-permute-done.17 = bf16[512,256]{1,0:T(8,128)(2,1)S(1)} collective-permute-done((bf16[512,256]{1,0:T(8,128)(2,1)}, bf16[512,256]{1,0:T(8,128)(2,1)S(1)}, u32[]{:S(2)}, u32[]{:S(2)}) %collective-permute-start.17) | collective-permute-done | bytes 262176 | tf_op jit(solution)/shard_map/ppermute | solution.py:226
  95.3 3.4 %collective-permute-start.18 = (bf16[512,256]{1,0:T(8,128)(2,1)}, bf16[512,256]{1,0:T(8,128)(2,1)S(1)}, u32[]{:S(2)}, u32[]{:S(2)}) collective-permute-start(bf16[512,256]{1,0:T(8,128)(2,1)} %get-tuple-element.52), channel_id=1, source_target_pairs={{0,4},{4,0},{8,12},{12,8},{16,20},{20,16},{24,28},{28,24},{1,5},{5... | collective-permute-start | bytes 786440 | tf_op jit(solution)/shard_map/ppermute | solution.py:230
  98.7 6.4 %collective-permute-done.18 = bf16[512,256]{1,0:T(8,128)(2,1)S(1)} collective-permute-done((bf16[512,256]{1,0:T(8,128)(2,1)}, bf16[512,256]{1,0:T(8,128)(2,1)S(1)}, u32[]{:S(2)}, u32[]{:S(2)}) %collective-permute-start.18) | collective-permute-done | bytes 262176 | tf_op jit(solution)/shard_map/ppermute | solution.py:230
  105.1 2.3 %collective-permute-start.19 = (bf16[512,256]{1,0:T(8,128)(2,1)}, bf16[512,256]{1,0:T(8,128)(2,1)S(1)}, u32[]{:S(2)}, u32[]{:S(2)}) collective-permute-start(bf16[512,256]{1,0:T(8,128)(2,1)} %get-tuple-element.53), channel_id=1, source_target_pairs={{0,4},{4,0},{8,12},{12,8},{16,20},{20,16},{24,28},{28,24},{1,5},{5... | collective-permute-start | bytes 786440 | tf_op jit(solution)/shard_map/ppermute | solution.py:230
  108.6 1.9 %collective-permute-start.20 = (bf16[512,256]{1,0:T(8,128)(2,1)S(1)}, bf16[512,256]{1,0:T(8,128)(2,1)S(1)}, u32[]{:S(2)}, u32[]{:S(2)}) collective-permute-start(bf16[512,256]{1,0:T(8,128)(2,1)S(1)} %fusion.7), channel_id=1, source_target_pairs={{8,0},{12,4},{16,8},{20,12},{24,16},{28,20},{9,1},{13,5},{17,9},{2... | collective-permute-start | bytes 786440 | tf_op jit(solution)/shard_map/ppermute | solution.py:226
  112.0 25.7 %collective-permute-done.20 = bf16[512,256]{1,0:T(8,128)(2,1)S(1)} collective-permute-done((bf16[512,256]{1,0:T(8,128)(2,1)S(1)}, bf16[512,256]{1,0:T(8,128)(2,1)S(1)}, u32[]{:S(2)}, u32[]{:S(2)}) %collective-permute-start.20) | collective-permute-done | bytes 262176 | tf_op jit(solution)/shard_map/ppermute | solution.py:226
  141.0 6.1 %collective-permute-done.21 = bf16[512,256]{1,0:T(8,128)(2,1)S(1)} collective-permute-done((bf16[512,256]{1,0:T(8,128)(2,1)S(1)}, bf16[512,256]{1,0:T(8,128)(2,1)S(1)}, u32[]{:S(2)}, u32[]{:S(2)}) %collective-permute-start.21) | collective-permute-done | bytes 262176 | tf_op jit(solution)/shard_map/ppermute | solution.py:226
  (77 shorter events, 24.3 us)
Async XLA Ops:
  0.6 4.8 %collective-permute-start.3 = (s32[1,128]{1,0:T(1,128)}, s32[1,128]{1,0:T(1,128)S(1)}, u32[]{:S(2)}, u32[]{:S(2)}) collective-permute-start(s32[1,128]{1,0:T(1,128)} %bitcast.6), channel_id=1, source_target_pairs={{0,1},{1,0},{2,3},{3,2},{4,5},{5,4},{6,7},{7,6},{8,9},{9,8},{10,11... | collective-permute-start | bytes 1544 | tf_op jit(solution)/shard_map/ppermute | solution.py:242
  1.9 16.8 %collective-permute-start = (bf16[512,256]{1,0:T(8,128)(2,1)S(1)}, bf16[512,256]{1,0:T(8,128)(2,1)S(1)}, u32[]{:S(2)}, u32[]{:S(2)}) collective-permute-start(bf16[512,256]{1,0:T(8,128)(2,1)S(1)} %pad_maximum_fusion.refs_7_), channel_id=1, source_target_pairs={{0,8},{4,12},{8,16},{12,20},{16,24},{20,28},{1,9},{5,13},{9,17},{1... | collective-permute-start | bytes 786440 | tf_op jit(solution)/shard_map/ppermute | solution.py:226
  6.2 3.6 %collective-permute-start.4 = (s32[2,128]{1,0:T(2,128)S(1)}, s32[2,128]{1,0:T(2,128)S(1)}, u32[]{:S(2)}, u32[]{:S(2)}) collective-permute-start(s32[2,128]{1,0:T(2,128)S(1)} %add_select_fusion.1), channel_id=1, source_target_pairs={{0,2},{1,3},{2,0},{3,1},{4,6},{5,7},{6,4},{7,5},{8,10},{9,11},{10,... | collective-permute-start | bytes 3080 | tf_op jit(solution)/shard_map/ppermute | solution.py:242
  9.7 8.6 %collective-permute-start.8 = (s32[512]{0:T(512)S(1)}, s32[512]{0:T(512)S(1)}, u32[]{:S(2)}, u32[]{:S(2)}) collective-permute-start(s32[512]{0:T(512)S(1)} %fusion.8), channel_id=1, source_target_pairs={{0,4},{4,8},{8,12},{12,16},{16,20},{20,24},{24,28},{1,5},{5,9},{9,... | collective-permute-start | bytes 6152 | tf_op jit(solution)/shard_map/ppermute | solution.py:226
  13.2 48.3 %copy-start.2 = (bf16[512,256]{1,0:T(8,128)(2,1)}, bf16[512,256]{1,0:T(8,128)(2,1)S(1)}, u32[]{:S(2)}) copy-start(bf16[512,256]{1,0:T(8,128)(2,1)S(1)} %pad_maximum_fusion.1.refs_9_) | copy-start | bytes 786436
  13.2 5.5 %collective-permute-start.7 = (s32[512]{0:T(512)S(1)}, s32[512]{0:T(512)S(1)}, u32[]{:S(2)}, u32[]{:S(2)}) collective-permute-start(s32[512]{0:T(512)S(1)} %fusion.8), channel_id=1, source_target_pairs={{0,8},{4,12},{8,16},{12,20},{16,24},{20,28},{1,9},{5,13},{9,17},{1... | collective-permute-start | bytes 6152 | tf_op jit(solution)/shard_map/ppermute | solution.py:226
  15.1 7.4 %collective-permute-start.6 = (s32[512]{0:T(512)S(1)}, s32[512]{0:T(512)S(1)}, u32[]{:S(2)}, u32[]{:S(2)}) collective-permute-start(s32[512]{0:T(512)S(1)} %fusion.8), channel_id=1, source_target_pairs={{0,12},{4,16},{8,20},{12,24},{16,28},{1,13},{5,17},{9,21},{13,25},... | collective-permute-start | bytes 6152 | tf_op jit(solution)/shard_map/ppermute | solution.py:226
  17.1 6.5 %collective-permute-start.5 = (s32[512]{0:T(512)S(1)}, s32[512]{0:T(512)S(1)}, u32[]{:S(2)}, u32[]{:S(2)}) collective-permute-start(s32[512]{0:T(512)S(1)} %fusion.8), channel_id=1, source_target_pairs={{0,16},{4,20},{8,24},{12,28},{1,17},{5,21},{9,25},{13,29},{2,18},{... | collective-permute-start | bytes 6152 | tf_op jit(solution)/shard_map/ppermute | solution.py:226
  18.7 9.1 %collective-permute-start.1 = (bf16[512,256]{1,0:T(8,128)(2,1)S(1)}, bf16[512,256]{1,0:T(8,128)(2,1)S(1)}, u32[]{:S(2)}, u32[]{:S(2)}) collective-permute-start(bf16[512,256]{1,0:T(8,128)(2,1)S(1)} %collective-permute-done.refs_5_), channel_id=1, source_target_pairs={{0,8},{4,12},{8,16},{12,20},{16,24},{20,28},{1,9},{5,13},{9,17},{1... | collective-permute-start | bytes 786440 | tf_op jit(solution)/shard_map/ppermute | solution.py:226
  20.7 7.1 %collective-permute-start.2 = (bf16[512,256]{1,0:T(8,128)(2,1)S(1)}, bf16[512,256]{1,0:T(8,128)(2,1)S(1)}, u32[]{:S(2)}, u32[]{:S(2)}) collective-permute-start(bf16[512,256]{1,0:T(8,128)(2,1)S(1)} %broadcast_select_fusion.1), channel_id=1, source_target_pairs={{0,4},{4,0},{8,12},{12,8},{16,20},{20,16},{24,28},{28,24},{1,5},{5... | collective-permute-start | bytes 786440 | tf_op jit(solution)/shard_map/ppermute | solution.py:230
  29.1 6.4 %collective-permute-start.9 = (bf16[512,256]{1,0:T(8,128)(2,1)S(1)}, bf16[512,256]{1,0:T(8,128)(2,1)S(1)}, u32[]{:S(2)}, u32[]{:S(2)}) collective-permute-start(bf16[512,256]{1,0:T(8,128)(2,1)S(1)} %broadcast_select_fusion), channel_id=1, source_target_pairs={{0,4},{4,0},{8,12},{12,8},{16,20},{20,16},{24,28},{28,24},{1,5},{5... | collective-permute-start | bytes 786440 | tf_op jit(solution)/shard_map/ppermute | solution.py:230
  29.5 8.3 %collective-permute-start.10 = (bf16[512,256]{1,0:T(8,128)(2,1)S(1)}, bf16[512,256]{1,0:T(8,128)(2,1)S(1)}, u32[]{:S(2)}, u32[]{:S(2)}) collective-permute-start(bf16[512,256]{1,0:T(8,128)(2,1)S(1)} %pad_maximum_fusion.1.refs_9_), channel_id=1, source_target_pairs={{0,8},{4,12},{8,16},{12,20},{16,24},{20,28},{1,9},{5,13},{9,17},{1... | collective-permute-start | bytes 786440 | tf_op jit(solution)/shard_map/ppermute | solution.py:226
  37.7 33.2 %collective-permute-start.12 = (bf16[512,256]{1,0:T(8,128)(2,1)S(1)}, bf16[512,256]{1,0:T(8,128)(2,1)S(1)}, u32[]{:S(2)}, u32[]{:S(2)}) collective-permute-start(bf16[512,256]{1,0:T(8,128)(2,1)S(1)} %collective-permute-done.10.refs_7_), channel_id=1, source_target_pairs={{0,4},{4,8},{8,12},{12,16},{16,20},{20,24},{24,28},{1,5},{5,9},{9,... | collective-permute-start | bytes 786440 | tf_op jit(solution)/shard_map/ppermute | solution.py:226
  41.4 31.8 %collective-permute-start.11 = (bf16[512,256]{1,0:T(8,128)(2,1)S(1)}, bf16[512,256]{1,0:T(8,128)(2,1)S(1)}, u32[]{:S(2)}, u32[]{:S(2)}) collective-permute-start(bf16[512,256]{1,0:T(8,128)(2,1)S(1)} %collective-permute-done.10.refs_7_), channel_id=1, source_target_pairs={{0,8},{4,12},{8,16},{12,20},{16,24},{20,28},{1,9},{5,13},{9,17},{1... | collective-permute-start | bytes 786440 | tf_op jit(solution)/shard_map/ppermute | solution.py:226
  43.4 25.6 %collective-permute-start.13 = (bf16[512,256]{1,0:T(8,128)(2,1)S(1)}, bf16[512,256]{1,0:T(8,128)(2,1)S(1)}, u32[]{:S(2)}, u32[]{:S(2)}) collective-permute-start(bf16[512,256]{1,0:T(8,128)(2,1)S(1)} %pad_maximum_fusion.1.refs_9_), channel_id=1, source_target_pairs={{0,4},{4,8},{8,12},{12,16},{16,20},{20,24},{24,28},{1,5},{5,9},{9,... | collective-permute-start | bytes 786440 | tf_op jit(solution)/shard_map/ppermute | solution.py:226
  61.5 28.4 %collective-permute-start.14 = (bf16[512,256]{1,0:T(8,128)(2,1)}, bf16[512,256]{1,0:T(8,128)(2,1)S(1)}, u32[]{:S(2)}, u32[]{:S(2)}) collective-permute-start(bf16[512,256]{1,0:T(8,128)(2,1)} %get-tuple-element.45), channel_id=1, source_target_pairs={{16,0},{20,4},{24,8},{28,12},{17,1},{21,5},{25,9},{29,13},{18,2},{... | collective-permute-start | bytes 786440 | tf_op jit(solution)/shard_map/ppermute | solution.py:226
  63.0 29.2 %collective-permute-start.15 = (bf16[512,256]{1,0:T(8,128)(2,1)}, bf16[512,256]{1,0:T(8,128)(2,1)S(1)}, u32[]{:S(2)}, u32[]{:S(2)}) collective-permute-start(bf16[512,256]{1,0:T(8,128)(2,1)} %get-tuple-element.46), channel_id=1, source_target_pairs={{12,0},{16,4},{20,8},{24,12},{28,16},{13,1},{17,5},{21,9},{25,13},... | collective-permute-start | bytes 786440 | tf_op jit(solution)/shard_map/ppermute | solution.py:226
  69.0 23.7 %collective-permute-start.16 = (bf16[512,256]{1,0:T(8,128)(2,1)}, bf16[512,256]{1,0:T(8,128)(2,1)S(1)}, u32[]{:S(2)}, u32[]{:S(2)}) collective-permute-start(bf16[512,256]{1,0:T(8,128)(2,1)} %get-tuple-element.47), channel_id=1, source_target_pairs={{8,0},{12,4},{16,8},{20,12},{24,16},{28,20},{9,1},{13,5},{17,9},{2... | collective-permute-start | bytes 786440 | tf_op jit(solution)/shard_map/ppermute | solution.py:226
  71.0 24.3 %collective-permute-start.17 = (bf16[512,256]{1,0:T(8,128)(2,1)}, bf16[512,256]{1,0:T(8,128)(2,1)S(1)}, u32[]{:S(2)}, u32[]{:S(2)}) collective-permute-start(bf16[512,256]{1,0:T(8,128)(2,1)} %get-tuple-element.48), channel_id=1, source_target_pairs={{4,0},{8,4},{12,8},{16,12},{20,16},{24,20},{28,24},{5,1},{9,5},{13... | collective-permute-start | bytes 786440 | tf_op jit(solution)/shard_map/ppermute | solution.py:226
  89.9 50.9 %copy-start.3 = (bf16[512,256]{1,0:T(8,128)(2,1)S(1)}, bf16[512,256]{1,0:T(8,128)(2,1)}, u32[]{:S(2)}) copy-start(bf16[512,256]{1,0:T(8,128)(2,1)} %get-tuple-element.44) | copy-start | bytes 786436
  95.3 9.9 %collective-permute-start.18 = (bf16[512,256]{1,0:T(8,128)(2,1)}, bf16[512,256]{1,0:T(8,128)(2,1)S(1)}, u32[]{:S(2)}, u32[]{:S(2)}) collective-permute-start(bf16[512,256]{1,0:T(8,128)(2,1)} %get-tuple-element.52), channel_id=1, source_target_pairs={{0,4},{4,0},{8,12},{12,8},{16,20},{20,16},{24,28},{28,24},{1,5},{5... | collective-permute-start | bytes 786440 | tf_op jit(solution)/shard_map/ppermute | solution.py:230
  105.1 6.9 %collective-permute-start.19 = (bf16[512,256]{1,0:T(8,128)(2,1)}, bf16[512,256]{1,0:T(8,128)(2,1)S(1)}, u32[]{:S(2)}, u32[]{:S(2)}) collective-permute-start(bf16[512,256]{1,0:T(8,128)(2,1)} %get-tuple-element.53), channel_id=1, source_target_pairs={{0,4},{4,0},{8,12},{12,8},{16,20},{20,16},{24,28},{28,24},{1,5},{5... | collective-permute-start | bytes 786440 | tf_op jit(solution)/shard_map/ppermute | solution.py:230
  108.6 29.2 %collective-permute-start.20 = (bf16[512,256]{1,0:T(8,128)(2,1)S(1)}, bf16[512,256]{1,0:T(8,128)(2,1)S(1)}, u32[]{:S(2)}, u32[]{:S(2)}) collective-permute-start(bf16[512,256]{1,0:T(8,128)(2,1)S(1)} %fusion.7), channel_id=1, source_target_pairs={{8,0},{12,4},{16,8},{20,12},{24,16},{28,20},{9,1},{13,5},{17,9},{2... | collective-permute-start | bytes 786440 | tf_op jit(solution)/shard_map/ppermute | solution.py:226
  138.9 8.3 %collective-permute-start.21 = (bf16[512,256]{1,0:T(8,128)(2,1)S(1)}, bf16[512,256]{1,0:T(8,128)(2,1)S(1)}, u32[]{:S(2)}, u32[]{:S(2)}) collective-permute-start(bf16[512,256]{1,0:T(8,128)(2,1)S(1)} %fusion.5), channel_id=1, source_target_pairs={{8,0},{12,4},{16,8},{20,12},{24,16},{28,20},{9,1},{13,5},{17,9},{2... | collective-permute-start | bytes 786440 | tf_op jit(solution)/shard_map/ppermute | solution.py:226
  (11 other events, 201.9 us)
